TPU v7x, 32 devices: a whole 2x2x4 slice. The times are simulated.
32 devices in a mesh: layer: 4 (over y, x), feat: 8 (over z, core).
Axes of the slice: x: 2, y: 2, z: 4, core: 2. Of those that a mesh axis runs over, the one named last changes fastest.
Arguments:
- source_decoder: bfloat16 [4, 1024, 8192], P('layer', 'feat'), may hold values from -0.0625 to 0.0625
- reader_encoder: bfloat16 [4, 8192, 6144], P('layer', None, 'feat'), may hold values from -6 to 6
- source_acts: bfloat16 [2048, 4096], P('feat', 'layer'), may hold values from 0 to 2
- target_grads: bfloat16 [2048, 24576], P('feat', 'layer'), may hold values from -0.13183594 to 0.13183594
- pair_source: int32 [4, 8, 24], P('layer', 'feat'), may hold values from 0 to 3
- pair_target: int32 [4, 8, 24], P('layer', 'feat'), may hold values from 0 to 5
- pair_count: int32 [4, 8], P('layer', 'feat'), may hold values from 1 to 24, as said below
Outputs:
- edge_table: float32 [4, 8, 24, 128, 128], P('layer', 'feat')
Inputs may be any that keep to these rules, and one draw needn't show every extreme that they name: `pair_count`: slots at and past the count of a reader layer and column are unused; in every draw some reader layer and column uses all 24 slots.
All inputs are finite; a program needn't handle non-finite values.
Results may differ from a plain program's by a relative error of at most 0.0003.
Values may be sent and summed in bfloat16 or wider, within the bound.
A program may use at most 192 MiB of HBM per device.

v0:
```python
import jax
import jax.numpy as jnp
from jax import lax
from jax.sharding import PartitionSpec as P


def local(
    source_decoder, reader_encoder, source_acts, target_grads, pair_source, pair_target, pair_count
):
    source_rows, target_rows = (
        lax.all_to_all(source_acts, "feat", split_axis=1, concat_axis=0, tiled=True),
        lax.all_to_all(target_grads, "feat", split_axis=1, concat_axis=0, tiled=True),
    )
    encoder = reader_encoder[0]
    block_size = source_decoder.shape[1]
    source_slab = source_rows[None]
    sources = pair_source[0, 0]
    targets = pair_target[0, 0]
    slot_count = sources.shape[0]
    live_count = pair_count[0, 0]
    panel_dec, panel_act = (
        lax.all_gather(source_decoder, "layer", axis=0, tiled=True),
        lax.all_gather(source_slab, "layer", axis=0, tiled=True),
    )

    def one_pair(slot_pos, edge_buffer):
        source = sources[slot_pos]
        target = targets[slot_pos]
        decoder_block = lax.dynamic_index_in_dim(panel_dec, source, 0, keepdims=False)
        enc_block = lax.dynamic_slice_in_dim(encoder, target * block_size, block_size, 1)
        virtual = jnp.dot(decoder_block, enc_block, preferred_element_type=jnp.float32)
        act_block = lax.dynamic_index_in_dim(panel_act, source, 0, keepdims=False)
        grad_block = lax.dynamic_slice_in_dim(target_rows, target * block_size, block_size, 1)
        coact = lax.dot_general(
            act_block, grad_block, (((0,), (0,)), ((), ())), preferred_element_type=jnp.float32
        )
        return lax.dynamic_update_index_in_dim(edge_buffer, virtual * coact, slot_pos, 0)

    edge_table = lax.fori_loop(
        0, live_count, one_pair, jnp.zeros((slot_count, block_size, block_size), jnp.float32)
    )
    return edge_table[None, None]


def solution(mesh):
    in_specs = (
        P("layer", "feat", None),
        P("layer", None, "feat"),
        P("feat", "layer"),
        P("feat", "layer"),
        P("layer", "feat", None),
        P("layer", "feat", None),
        P("layer", "feat"),
    )
    out_specs = P("layer", "feat", None, None, None)
    return jax.shard_map(local, mesh=mesh, in_specs=in_specs, out_specs=out_specs, check_vma=False)
```

profile of v0, /device:TPU:5, one launch (start us, length us, event | category | flops | bytes accessed | tf_op | source)
XLA Modules:
  0.0 375.2 jit_solution(6197434539734011829)
XLA Ops:
  6.5 1.0 copy-done
  7.7 19.8 %all_to_all.35 = bf16[256,8,128]{2,0,1:T(8,128)(2,1)} all-to-all(bf16[256,8,128]{2,0,1:T(8,128)(2,1)S(1)} %copy_bitcast_fusion.1), channel_id=1, replica_groups=mesh['layer'=4,'feat'=8] {'feat'}, dimensions={1} | all-to-all | bytes 1048576 | tf_op jit(solution)/shard_map/all_to_all | solution.py:11
  27.5 0.7 all-gather.3.cloned.1.call-update
  28.2 3.8 %copy.16 = bf16[32,8,8,768]{3,2,0,1:T(8,128)(2,1)} copy(bf16[32,8,8,768]{3,2,1,0:T(8,128)(2,1)} %bitcast.44) | data formatting | bytes 6291456 | tf_op jit(solution)/shard_map/all_to_all | solution.py:12
  32.1 5.5 %all-to-all-start.1 = ((bf16[256,8,768]{2,0,1:T(8,128)(2,1)}), bf16[256,8,768]{2,0,1:T(8,128)(2,1)}, u32[]{:S(2)}, u32[]{:S(2)}) async-start(bf16[256,8,768]{2,0,1:T(8,128)(2,1)} %bitcast.42), calls=%async_computation.1 | async-start | bytes 6291456 | tf_op jit(solution)/shard_map/all_to_all | solution.py:12
  37.6 24.6 %all-gather.5.cloned.1.call-done = bf16[4,2048,128]{2,1,0:T(8,128)(2,1)} async-done(((bf16[1,2048,128]{2,1,0:T(8,128)(2,1)}), bf16[4,2048,128]{2,1,0:T(8,128)(2,1)}) %all-gather.5.cloned.1.call-update) | async-done | bytes 2097168 | tf_op jit(solution)/shard_map/all_gather | solution.py:23
  62.2 46.2 %all-to-all-done.1 = bf16[256,8,768]{2,0,1:T(8,128)(2,1)} async-done(((bf16[256,8,768]{2,0,1:T(8,128)(2,1)}), bf16[256,8,768]{2,0,1:T(8,128)(2,1)}, u32[]{:S(2)}, u32[]{:S(2)}) %all-to-all-start.1) | async-done | bytes 3145760 | tf_op jit(solution)/shard_map/all_to_all | solution.py:12
  108.4 43.3 %all-gather.3.cloned.1.call-done = bf16[4,128,8192]{2,1,0:T(8,128)(2,1)} async-done(((bf16[1,128,8192]{2,1,0:T(8,128)(2,1)}), bf16[4,128,8192]{2,1,0:T(8,128)(2,1)}) %all-gather.3.cloned.1.call-update) | async-done | bytes 8388624 | tf_op jit(solution)/shard_map/all_gather | solution.py:22
  151.8 215.3 %while.10 = (s32[]{:T(128)}, f32[24,128,128]{2,1,0:T(8,128)S(1)}, s32[]{:T(128)}, s32[24]{0:T(128)S(1)}, bf16[4,128,8192]{2,1,0:T(8,128)(2,1)}, /*index=5*/s32[2...) while((s32[]{:T(128)}, f32[24,128,128]{2,1,0:T(8,128)S(1)}, ...), condition=%wide.region_1.2_spmd, body=%wide.region_0.1_spmd.sunk | while | flops 335560704 | bytes 5439787 | solution.py:39
  155.0 0.7 dynamic_slice.42
  156.3 2.9 fusion.22
  159.2 1.5 fusion.23
  164.0 0.7 dynamic_slice.42
  165.2 2.9 fusion.22
  168.2 1.6 fusion.23
  173.0 0.7 dynamic_slice.42
  174.2 2.9 fusion.22
  177.2 1.5 fusion.23
  181.9 0.7 dynamic_slice.42
  183.2 2.9 fusion.22
  186.1 1.5 fusion.23
  190.8 0.7 dynamic_slice.42
  192.1 2.9 fusion.22
  195.0 1.5 fusion.23
  199.8 0.7 dynamic_slice.42
  201.1 2.9 fusion.22
  204.0 1.5 fusion.23
  210.0 2.9 fusion.22
  212.9 1.5 fusion.23
  218.9 2.9 fusion.22
  221.9 1.5 fusion.23
  227.9 2.9 fusion.22
  230.8 1.5 fusion.23
  236.8 2.9 fusion.22
  239.8 1.5 fusion.23
  245.8 2.9 fusion.22
  248.7 1.5 fusion.23
  254.7 2.9 fusion.22
  257.7 1.5 fusion.23
  263.7 2.9 fusion.22
  266.6 1.5 fusion.23
  272.6 2.9 fusion.22
  275.5 1.5 fusion.23
  281.6 2.9 fusion.22
  284.5 1.5 fusion.23
  290.5 2.9 fusion.22
  293.4 1.5 fusion.23
  299.4 2.9 fusion.22
  302.4 1.5 fusion.23
  308.4 2.9 fusion.22
  311.3 1.5 fusion.23
  317.3 2.9 fusion.22
  320.3 1.5 fusion.23
  326.3 2.9 fusion.22
  329.2 1.5 fusion.23
  335.2 2.9 fusion.22
  338.1 1.5 fusion.23
  344.2 2.9 fusion.22
  347.1 1.5 fusion.23
  353.1 2.9 fusion.22
  356.0 1.5 fusion.23
  362.0 2.9 fusion.22
  365.0 1.5 fusion.23
  367.2 1.1 copy-done.1
  (53 shorter events, 27.6 us)
Async XLA Ops:
  6.5 1.0 copy-start
  6.5 55.6 %all-gather.5.cloned.1.call-start = ((), (), s32[]{:S(2)}) async-start(), calls=%async_computation.3 | async-start | bytes 2621440 | tf_op jit(solution)/shard_map/all_gather | solution.py:23
  27.5 124.2 %all-gather.3.cloned.1.call-start = ((), (), s32[]{:S(2)}) async-start(), calls=%async_computation.2 | async-start | bytes 10485760 | tf_op jit(solution)/shard_map/all_gather | solution.py:22
  32.0 119.8 %copy-start.2 = (s32[1,1,24]{2,1,0:T(1,128)S(1)}, s32[1,1,24]{2,1,0:T(1,128)}, u32[]{:S(2)}) copy-start(s32[1,1,24]{2,1,0:T(1,128)} %param.13) | copy-start | bytes 292
  32.1 119.8 %copy-start.3 = (s32[1,1,24]{2,1,0:T(1,128)S(1)}, s32[1,1,24]{2,1,0:T(1,128)}, u32[]{:S(2)}) copy-start(s32[1,1,24]{2,1,0:T(1,128)} %param.14) | copy-start | bytes 292
  32.1 76.3 %all-to-all-start.1 = ((bf16[256,8,768]{2,0,1:T(8,128)(2,1)}), bf16[256,8,768]{2,0,1:T(8,128)(2,1)}, u32[]{:S(2)}, u32[]{:S(2)}) async-start(bf16[256,8,768]{2,0,1:T(8,128)(2,1)} %bitcast.42), calls=%async_computation.1 | async-start | bytes 6291456 | tf_op jit(solution)/shard_map/all_to_all | solution.py:12
  367.2 1.1 copy-start.1
Sparse Core Ops, SparseCore 0:
  27.6 34.5 all-gather.4
  64.0 87.5 all-gather.2
where the time goes:
time: 377 us; the launch traced here: 375 us
  waiting for transfers between devices  115 us (31%)
  matrix products  107 us (28%)
  loops' own time  76.8 us (20%)
  local copies, waits for them, and re-layouts  37.4 us (10%)
  blocking collectives  19.8 us (5%)
  between operations  13.5 us (4%)
  starting transfers between devices  5.58 us (1%)
    another operation x1, loops' own time, local(): lax.fori_loop(0, live_count, one_pair, jnp.zeros((slot_count, block_size,...  76.8 us
    dot_general x24, matrix products, one_pair(): jnp.dot(decoder_block, enc_block, preferred_element_type=jnp.float32)  70.2 us
    all_to_all x1, waiting for transfers between devices, local(): lax.all_to_all(target_grads, 'feat', split_axis=1, concat_axis=0, tiled=T...  46.2 us
    all_gather x1, waiting for transfers between devices, local(): lax.all_gather(source_decoder, 'layer', axis=0, tiled=True)  43.3 us
    dot_general x24, matrix products, one_pair(): lax.dot_general(act_block, grad_block, (((0,), (0,)), ((), ())), preferre...  37.2 us
    all_gather x1, waiting for transfers between devices, local(): lax.all_gather(source_slab, 'layer', axis=0, tiled=True)  24.6 us
    all_to_all x1, blocking collectives, local(): lax.all_to_all(source_acts, 'feat', split_axis=1, concat_axis=0, tiled=True)  19.8 us
    dynamic_slice x24, local copies, waits for them, and re-layouts, one_pair(): target = targets[slot_pos]  15.6 us
  transfers between devices with their start and end apart: 3, of which 3 were waited for; matrix products, arithmetic and copies ran while one was open for 1% of the time, Pallas kernels for 0%

commit v1 on v0

--- a/solution.py
+++ b/solution.py
@@ -1,7 +1,40 @@
+import functools
 import jax
 import jax.numpy as jnp
 from jax import lax
 from jax.sharding import PartitionSpec as P
+
+
+def try_all_the_field(obj, net_axis):
+    mid_arr = lax.axis_size(net_axis)
+    placed, reached, a_now = (mid_arr, lax.axis_index(net_axis), obj.shape[0])
+    w_next = lax.dynamic_update_slice_in_dim(
+        jnp.zeros(
+            [b * placed if src_i == 0 else b for src_i, b in enumerate(obj.shape)], obj.dtype
+        ),
+        obj,
+        reached * a_now,
+        axis=0,
+    )
+    side_arr = b_now = obj
+    for it in range(1, placed // 2 + 1):
+        side_arr = lax.ppermute(
+            side_arr, net_axis, [(src_i, (src_i + 1) % placed) for src_i in range(placed)]
+        )
+        w_next = lax.dynamic_update_slice_in_dim(
+            w_next, side_arr, (reached - it) % placed * a_now, axis=0
+        )
+        if 2 * it < placed:
+            b_now = lax.ppermute(
+                b_now, net_axis, [(src_i, (src_i - 1) % placed) for src_i in range(placed)]
+            )
+            w_next = lax.dynamic_update_slice_in_dim(
+                w_next, b_now, (reached + it) % placed * a_now, axis=0
+            )
+    return w_next
+
+
+guide_quotas = functools.partial(try_all_the_field, net_axis="layer")
 
 
 def local(
@@ -19,7 +52,7 @@
     slot_count = sources.shape[0]
     live_count = pair_count[0, 0]
     panel_dec, panel_act = (
-        lax.all_gather(source_decoder, "layer", axis=0, tiled=True),
+        guide_quotas(source_decoder),
         lax.all_gather(source_slab, "layer", axis=0, tiled=True),
     )
 

time: 377 us -> 398 us (1.056)
  blocking collectives: 19.8 us -> 0 us
  waiting for transfers between devices: 115 us -> 131 us
  local copies, waits for them, and re-layouts: 37.4 us -> 51.1 us
  starting transfers between devices: 5.58 us -> 13.5 us
    ppermute x0 -> x3, waiting for transfers between devices: none -> 121 us  [the longest x2 75.2 us: try_all_the_field(): lax.ppermute(side_arr, net_axis, [(src_i, (src_i + 1) % placed) for src_i...]
    all_to_all x1, waiting for transfers between devices: 46.2 us -> 0.01 us  [local(): lax.all_to_all(target_grads, 'feat', split_axis=1, concat_axis=0, tiled=T...]
    all_gather x1 -> x0, waiting for transfers between devices: 43.3 us -> none  [local(): lax.all_gather(source_decoder, 'layer', axis=0, tiled=True)]
    all_gather x1, waiting for transfers between devices: 24.6 us -> 0.01 us  [local(): lax.all_gather(source_slab, 'layer', axis=0, tiled=True)]
    all_to_all x1 -> x0, blocking collectives: 19.8 us -> none  [local(): lax.all_to_all(source_acts, 'feat', split_axis=1, concat_axis=0, tiled=True)]
    dynamic_update_slice x0 -> x4, local copies, waits for them, and re-layouts: none -> 10.8 us  [the longest x2 6.21 us: try_all_the_field(): lax.dynamic_update_slice_in_dim(w_next, side_arr, (reached - it) % placed...]
    all_to_all x0 -> x1, waiting for transfers between devices: none -> 9.55 us  [local(): lax.all_to_all(source_acts, 'feat', split_axis=1, concat_axis=0, tiled=True)]
    all_to_all x0 -> x1, starting transfers between devices: none -> 5.55 us  [local(): lax.all_to_all(source_acts, 'feat', split_axis=1, concat_axis=0, tiled=True)]
  transfers between devices with their start and end apart: 3 -> 6, of which waited for: 3 -> 4; matrix products, arithmetic and copies ran while one was open for 1% -> 5% of each run, Pallas kernels for 0% -> 0%
where the time goes in v1:
time: 398 us; the launch traced here: 395 us
  waiting for transfers between devices  131 us (33%)
  matrix products  107 us (27%)
  loops' own time  79.4 us (20%)
  local copies, waits for them, and re-layouts  51.1 us (13%)
  starting transfers between devices  13.5 us (3%)
  between operations  13.4 us (3%)
    another operation x1, loops' own time, local(): lax.fori_loop(0, live_count, one_pair, jnp.zeros((slot_count, block_size,...  79.4 us
    ppermute x2, waiting for transfers between devices, try_all_the_field(): lax.ppermute(side_arr, net_axis, [(src_i, (src_i + 1) % placed) for src_i...  75.2 us
    dot_general x24, matrix products, one_pair(): jnp.dot(decoder_block, enc_block, preferred_element_type=jnp.float32)  70.2 us
    ppermute x1, waiting for transfers between devices, try_all_the_field(): lax.ppermute(b_now, net_axis, [(src_i, (src_i - 1) % placed) for src_i in...  45.8 us
    dot_general x24, matrix products, one_pair(): lax.dot_general(act_block, grad_block, (((0,), (0,)), ((), ())), preferre...  37.1 us
    dynamic_slice x24, local copies, waits for them, and re-layouts, one_pair(): target = targets[slot_pos]  14.1 us
    dynamic_slice x24, local copies, waits for them, and re-layouts, one_pair(): source = sources[slot_pos]  14.1 us
    all_to_all x1, waiting for transfers between devices, local(): lax.all_to_all(source_acts, 'feat', split_axis=1, concat_axis=0, tiled=True)  9.55 us
  transfers between devices with their start and end apart: 6, of which 4 were waited for; matrix products, arithmetic and copies ran while one was open for 5% of the time, Pallas kernels for 0%

profile of v1, /device:TPU:5, one launch (start us, length us, event | category | flops | bytes accessed | tf_op | source)
XLA Modules:
  0.0 395.4 jit_solution(883295884212652990)
XLA Ops:
  8.5 5.5 %all-to-all-start = ((bf16[256,8,128]{2,0,1:T(8,128)(2,1)}), bf16[256,8,128]{2,0,1:T(8,128)(2,1)S(1)}, u32[]{:S(2)}, u32[]{:S(2)}) async-start(bf16[256,8,128]{2,0,1:T(8,128)(2,1)} %copy_bitcast_fusion.1), calls=%async_computation | async-start | bytes 1048576 | tf_op jit(solution)/shard_map/all_to_all | solution.py:44
  14.0 1.2 collective-permute-start
  15.2 3.8 copy.16
  19.1 9.6 %all-to-all-done = bf16[256,8,128]{2,0,1:T(8,128)(2,1)S(1)} async-done(((bf16[256,8,128]{2,0,1:T(8,128)(2,1)}), bf16[256,8,128]{2,0,1:T(8,128)(2,1)S(1)}, u32[]{:S(2)}, u32[]{:S(2)}) %all-to-all-start) | async-done | bytes 524320 | tf_op jit(solution)/shard_map/all_to_all | solution.py:44
  29.4 5.2 %all-to-all-start.1 = ((bf16[256,8,768]{2,0,1:T(8,128)(2,1)}), bf16[256,8,768]{2,0,1:T(8,128)(2,1)}, u32[]{:S(2)}, u32[]{:S(2)}) async-start(bf16[256,8,768]{2,0,1:T(8,128)(2,1)} %bitcast.42), calls=%async_computation.1 | async-start | bytes 6291456 | tf_op jit(solution)/shard_map/all_to_all | solution.py:45
  34.6 1.2 collective-permute-start.1
  35.9 32.5 %collective-permute-done = bf16[1,128,8192]{2,1,0:T(8,128)(2,1)} collective-permute-done((bf16[1,128,8192]{2,1,0:T(8,128)(2,1)}, bf16[1,128,8192]{2,1,0:T(8,128)(2,1)}, u32[]{:S(2)}, u32[]{:S(2)}) %collective-permute-start) | collective-permute-done | bytes 2097184 | tf_op jit(solution)/shard_map/ppermute | solution.py:21
  68.7 4.2 %broadcast_in_dim.17 = bf16[4,128,8192]{2,1,0:T(8,128)(2,1)} broadcast(bf16[]{:T(256)} %constant.55.clone.1), dimensions={} | broadcast | bytes 8388610 | tf_op jit(solution)/shard_map/broadcast_in_dim | solution.py:12
  72.9 1.5 constant_dynamic-update-slice_fusion.3
  74.4 3.1 constant_dynamic-update-slice_fusion.2
  77.5 45.8 %collective-permute-done.1 = bf16[1,128,8192]{2,1,0:T(8,128)(2,1)} collective-permute-done((bf16[1,128,8192]{2,1,0:T(8,128)(2,1)S(1)}, bf16[1,128,8192]{2,1,0:T(8,128)(2,1)}, u32[]{:S(2)}, u32[]{:S(2)}) %collective-permute-start.1) | collective-permute-done | bytes 2097184 | tf_op jit(solution)/shard_map/ppermute | solution.py:28
  123.3 3.1 constant_dynamic-update-slice_fusion.1
  126.5 42.8 %collective-permute-done.2 = bf16[1,128,8192]{2,1,0:T(8,128)(2,1)} collective-permute-done((bf16[1,128,8192]{2,1,0:T(8,128)(2,1)}, bf16[1,128,8192]{2,1,0:T(8,128)(2,1)}, u32[]{:S(2)}, u32[]{:S(2)}) %collective-permute-start.2) | collective-permute-done | bytes 2097184 | tf_op jit(solution)/shard_map/ppermute | solution.py:21
  169.2 3.1 constant_dynamic-update-slice_fusion
  172.5 214.9 %while.10 = (s32[]{:T(128)}, f32[24,128,128]{2,1,0:T(8,128)S(1)}, s32[]{:T(128)}, s32[24]{0:T(128)S(1)}, bf16[4,128,8192]{2,1,0:T(8,128)(2,1)}, /*index=5*/s32[2...) while((s32[]{:T(128)}, f32[24,128,128]{2,1,0:T(8,128)S(1)}, ...), condition=%wide.region_1.2_spmd, body=%wide.region_0.1_spmd.sunk | while | flops 335560704 | bytes 5439787 | solution.py:72
  177.0 2.9 fusion.22
  179.9 1.5 fusion.23
  185.9 2.9 fusion.22
  188.8 1.5 fusion.23
  194.8 2.9 fusion.22
  197.8 1.5 fusion.23
  203.8 2.9 fusion.22
  206.7 1.5 fusion.23
  212.7 2.9 fusion.22
  215.6 1.5 fusion.23
  221.6 2.9 fusion.22
  224.5 1.5 fusion.23
  230.5 2.9 fusion.22
  233.5 1.5 fusion.23
  239.5 2.9 fusion.22
  242.4 1.5 fusion.23
  248.4 2.9 fusion.22
  251.3 1.5 fusion.23
  257.3 2.9 fusion.22
  260.2 1.5 fusion.23
  266.2 2.9 fusion.22
  269.2 1.5 fusion.23
  275.2 2.9 fusion.22
  278.1 1.5 fusion.23
  284.1 2.9 fusion.22
  287.0 1.5 fusion.23
  293.0 2.9 fusion.22
  295.9 1.5 fusion.23
  301.9 2.9 fusion.22
  304.9 1.5 fusion.23
  310.9 2.9 fusion.22
  313.8 1.5 fusion.23
  319.8 2.9 fusion.22
  322.7 1.5 fusion.23
  328.7 2.9 fusion.22
  331.7 1.5 fusion.23
  337.6 2.9 fusion.22
  340.6 1.5 fusion.23
  346.6 2.9 fusion.22
  349.5 1.5 fusion.23
  355.5 2.9 fusion.22
  358.4 1.5 fusion.23
  364.4 2.9 fusion.22
  367.4 1.5 fusion.23
  373.4 2.9 fusion.22
  376.3 1.5 fusion.23
  382.3 2.9 fusion.22
  385.2 1.5 fusion.23
  387.4 1.1 copy-done.3
  (66 shorter events, 31.4 us)
Async XLA Ops:
  6.5 1.0 copy-start
  8.5 20.1 %all-to-all-start = ((bf16[256,8,128]{2,0,1:T(8,128)(2,1)}), bf16[256,8,128]{2,0,1:T(8,128)(2,1)S(1)}, u32[]{:S(2)}, u32[]{:S(2)}) async-start(bf16[256,8,128]{2,0,1:T(8,128)(2,1)} %copy_bitcast_fusion.1), calls=%async_computation | async-start | bytes 1048576 | tf_op jit(solution)/shard_map/all_to_all | solution.py:44
  14.0 54.3 %collective-permute-start = (bf16[1,128,8192]{2,1,0:T(8,128)(2,1)}, bf16[1,128,8192]{2,1,0:T(8,128)(2,1)}, u32[]{:S(2)}, u32[]{:S(2)}) collective-permute-start(bf16[1,128,8192]{2,1,0:T(8,128)(2,1)} %param.9), channel_id=1, source_target_pairs={{0,8},{8,16},{16,24},{24,0},{1,9},{9,17},{17,25},{25,1},{2,10},{10... | collective-permute-start | bytes 6291464 | tf_op jit(solution)/shard_map/ppermute | solution.py:21
  28.6 0.8 copy-start.2
  28.6 6.0 %copy-start.1 = (bf16[1,128,8192]{2,1,0:T(8,128)(2,1)S(1)}, bf16[1,128,8192]{2,1,0:T(8,128)(2,1)}, u32[]{:S(2)}) copy-start(bf16[1,128,8192]{2,1,0:T(8,128)(2,1)} %param.9) | copy-start | bytes 6291460
  29.4 142.9 %all-to-all-start.1 = ((bf16[256,8,768]{2,0,1:T(8,128)(2,1)}), bf16[256,8,768]{2,0,1:T(8,128)(2,1)}, u32[]{:S(2)}, u32[]{:S(2)}) async-start(bf16[256,8,768]{2,0,1:T(8,128)(2,1)} %bitcast.42), calls=%async_computation.1 | async-start | bytes 6291456 | tf_op jit(solution)/shard_map/all_to_all | solution.py:45
  34.6 137.7 %all-gather.2.cloned.1.call-start = ((), (), s32[]{:S(2)}) async-start(), calls=%async_computation.2 | async-start | bytes 2621440 | tf_op jit(solution)/shard_map/all_gather | solution.py:56
  34.6 88.7 %collective-permute-start.1 = (bf16[1,128,8192]{2,1,0:T(8,128)(2,1)S(1)}, bf16[1,128,8192]{2,1,0:T(8,128)(2,1)}, u32[]{:S(2)}, u32[]{:S(2)}) collective-permute-start(bf16[1,128,8192]{2,1,0:T(8,128)(2,1)S(1)} %copy-done.1), channel_id=1, source_target_pairs={{0,24},{8,0},{16,8},{24,16},{1,25},{9,1},{17,9},{25,17},{2,26},{10... | collective-permute-start | bytes 6291464 | tf_op jit(solution)/shard_map/ppermute | solution.py:28
  68.4 100.9 %collective-permute-start.2 = (bf16[1,128,8192]{2,1,0:T(8,128)(2,1)}, bf16[1,128,8192]{2,1,0:T(8,128)(2,1)}, u32[]{:S(2)}, u32[]{:S(2)}) collective-permute-start(bf16[1,128,8192]{2,1,0:T(8,128)(2,1)} %collective-permute-done), channel_id=1, source_target_pairs={{0,8},{8,16},{16,24},{24,0},{1,9},{9,17},{17,25},{25,1},{2,10},{10... | collective-permute-start | bytes 6291464 | tf_op jit(solution)/shard_map/ppermute | solution.py:21
  126.5 46.0 %copy-start.4 = (s32[1,1,24]{2,1,0:T(1,128)S(1)}, s32[1,1,24]{2,1,0:T(1,128)}, u32[]{:S(2)}) copy-start(s32[1,1,24]{2,1,0:T(1,128)} %param.13) | copy-start | bytes 292
  126.5 46.1 %copy-start.5 = (s32[1,1,24]{2,1,0:T(1,128)S(1)}, s32[1,1,24]{2,1,0:T(1,128)}, u32[]{:S(2)}) copy-start(s32[1,1,24]{2,1,0:T(1,128)} %param.14) | copy-start | bytes 292
  387.4 1.1 copy-start.3
Sparse Core Ops, SparseCore 0:
  37.3 53.1 all-gather.1
